TPU v7x, 128 devices: a whole 4x4x4 slice. The times are simulated.
128 devices in a mesh: dp: 8 (over y, core), ctx: 16 (over x, z).
Axes of the slice: x: 4, y: 4, z: 4, core: 2. Of those that a mesh axis runs over, the one named last changes fastest.
Arguments:
- features: bfloat16 [8, 2048, 4096], P('dp', 'ctx'), may hold values from -6 to 6
- queries: bfloat16 [8, 2048, 4096], P('dp', 'ctx'), may hold values from -100 to 100
- keys: bfloat16 [8, 2048, 1024], P('dp', 'ctx'), may hold values from -4 to 4
- values: bfloat16 [8, 2048, 1024], P('dp', 'ctx'), may hold values from -6 to 6
- grad_out: bfloat16 [8, 2048, 4096], P('dp', 'ctx'), may hold values from -6 to 6
- lengths: int32 [8], P('dp'), may hold values from 512 to 2048, as said below
- placement: int32 [8, 16], P('dp'), may hold values from 0 to 15, as said below
- query_down: bfloat16 [4096, 16], replicated, may hold values from -0.09375 to 0.09375
- query_up: bfloat16 [16, 4096], replicated, may hold values from -1.5 to 1.5
- value_down: bfloat16 [4096, 16], replicated, may hold values from -0.09375 to 0.09375
- value_up: bfloat16 [16, 1024], replicated, may hold values from -1.5 to 1.5
Outputs:
- grad_query: bfloat16 [8, 2048, 4096], P('dp', 'ctx')
- grad_key: bfloat16 [8, 2048, 1024], P('dp', 'ctx')
- grad_value: bfloat16 [8, 2048, 1024], P('dp', 'ctx')
- query_down_gradient: float32 [4096, 16], replicated
- query_up_gradient: float32 [16, 4096], replicated
- value_down_gradient: float32 [4096, 16], replicated
- value_up_gradient: float32 [16, 1024], replicated
Inputs may be any that keep to these rules, and one draw needn't show every extreme that they name: `lengths`: some chain has all 2048 positions live. `placement`: each row is a permutation of the tiles of a chain.
All inputs are finite; a program needn't handle non-finite values.
Results may differ from a plain program's by a relative error of at most 0.01.
Values may be sent and summed in bfloat16 or wider, within the bound.
No kernel may reach another device: no remote copies, remote signals or barrier semaphores. Data moves between devices by JAX's collectives and lax.ppermute only.
A program may use at most 192 MiB of HBM per device.

v0:
```python
import math

import jax
import jax.numpy as jnp
import numpy as np
from jax import lax
from jax.experimental import pallas as pl
from jax.experimental.pallas import tpu as pltpu
from jax.sharding import PartitionSpec as P

D = 4096
H = 32
KVH = 8
DH = 128
R = 16
TILE = 128
TILES = 16
WINDOW = TILE * TILES
DEVICES = 128
DP = 8
SCALE = 1.0 / math.sqrt(DH)
LOG2E = math.log2(math.e)
ADAPTER_SCALING = 2.0
FAR_BELOW = -1e30
IN_ROWS = 6 * TILE + 2 * R
OUT_ROWS = 4 * TILE + 2 * R
PIECE = 7 * R
PARTS = 4
PACK_COPIES = 3 * PARTS + 6
QB = 256
KB = 256
BLOCKS = WINDOW // QB

F32 = jnp.float32
BF16 = jnp.bfloat16
VMEM = pl.BlockSpec(memory_space=pltpu.VMEM)
SMEM = pl.BlockSpec(memory_space=pltpu.SMEM)
HBM = pl.BlockSpec(memory_space=pltpu.HBM)


def nt(a, b):
    return lax.dot_general(a, b, (((1,), (1,)), ((), ())), preferred_element_type=F32)


def nn(a, b):
    return lax.dot_general(a, b, (((1,), (0,)), ((), ())), preferred_element_type=F32)


def params(mebibytes):
    return pltpu.CompilerParams(vmem_limit_bytes=mebibytes * 1024 * 1024)


def pack_kernel(
    info,
    features,
    queries,
    keys,
    values,
    grad_out,
    q_down,
    v_down,
    out,
    f_in,
    q_in,
    k_in,
    v_in,
    g_in,
    qd_in,
    vd_in,
    held,
    sems,
):
    used = iter(range(PACK_COPIES))

    def copy(source, target):
        made = pltpu.make_async_copy(source, target, sems.at[next(used)])
        made.start()
        return made

    width = D // PARTS
    some = TILES // PARTS
    waits = [copy(keys, k_in), copy(values, v_in)]
    parts = []
    for p in range(PARTS):
        at = slice(p * width, p * width + width)
        parts.append(
            (copy(queries.at[:, at], q_in.at[:, at]), copy(grad_out.at[:, at], g_in.at[:, at]))
        )
    low = [copy(features, f_in), copy(q_down, qd_in), copy(v_down, vd_in)]
    for made in waits:
        made.wait()
    sent = []
    for p in range(PARTS):
        for made in parts[p]:
            made.wait()
        for j in range(p * some, p * some + some):
            h = j // 2
            held[j, 0:128] = q_in[:, j * 256 : j * 256 + 128]
            held[j, 128:256] = q_in[:, j * 256 + 128 : j * 256 + 256]
            held[j, 256:384] = g_in[:, j * 256 : j * 256 + 128]
            held[j, 384:512] = g_in[:, j * 256 + 128 : j * 256 + 256]
            held[j, 512:640] = k_in[:, h * 128 : h * 128 + 128]
            held[j, 640:768] = v_in[:, h * 128 : h * 128 + 128]
        at = pl.ds(p * some, some), pl.ds(0, 6 * TILE)
        sent.append(copy(held.at[at], out.at[at]))
    for made in low:
        made.wait()
    low_q = nt(qd_in[...], f_in[...]).astype(BF16)
    low_v = nt(vd_in[...], f_in[...]).astype(BF16)
    for j in range(TILES):
        held[j, 768:784] = low_q
        held[j, 784:800] = low_v
    at = pl.ds(0, TILES), pl.ds(6 * TILE, 2 * R)
    sent.append(copy(held.at[at], out.at[at]))
    for made in sent:
        made.wait()


def pack(info, features, queries, keys, values, grad_out, q_down, v_down):
    return pl.pallas_call(
        pack_kernel,
        out_shape=jax.ShapeDtypeStruct((TILES, IN_ROWS, 128), BF16),
        in_specs=[SMEM] + [HBM] * 7,
        out_specs=HBM,
        scratch_shapes=[
            pltpu.VMEM((TILE, D), BF16),
            pltpu.VMEM((TILE, D), BF16),
            pltpu.VMEM((TILE, KVH * DH), BF16),
            pltpu.VMEM((TILE, KVH * DH), BF16),
            pltpu.VMEM((TILE, D), BF16),
            pltpu.VMEM((R, D), BF16),
            pltpu.VMEM((R, D), BF16),
            pltpu.VMEM((TILES, IN_ROWS, 128), BF16),
            pltpu.SemaphoreType.DMA((PACK_COPIES,)),
        ],
        compiler_params=params(56),
        name="pack",
    )(info, features, queries, keys, values, grad_out, q_down, v_down)


def rotary(tables, tile, count):
    cos_r, sin_r = tables[0:64], tables[64:128]
    cosine, sine = [], []
    for t in range(tile, tile + count):
        cos_t, sin_t = tables[128:192, t : t + 1], tables[192:256, t : t + 1]
        cosine.append(cos_t * cos_r - sin_t * sin_r)
        sine.append(sin_t * cos_r + cos_t * sin_r)
    return jnp.concatenate(cosine, 1), jnp.concatenate(sine, 1)


def attention_kernel(
    place,
    info,
    recv,
    q_up,
    v_up,
    tables,
    out,
    up_out,
    qs,
    gs,
    ks,
    vs,
    kt,
    low,
    s_all,
    dp_all,
    dk,
    dv,
    inner,
    pre,
    upg,
    inv,
):
    here = info[0]
    length = info[1]
    rows = lax.broadcasted_iota(jnp.int32, (TILE, 128), 0)

    def arrange(t, _):
        p = place[t]
        inv[p] = t
        block = p // 2
        offset = pl.multiple_of((p % 2) * TILE, TILE)
        at = pl.ds(pl.multiple_of(p * TILE, TILE), TILE)
        live = rows + p * TILE < length
        for h in range(2):
            to = pl.ds(pl.multiple_of(h * QB + offset, TILE), TILE)
            qs[block, to] = recv[t, h * 128 : h * 128 + 128]
            grad = recv[t, 256 + h * 128 : 384 + h * 128].astype(F32)
            gs[block, to] = jnp.where(live, grad, 0.0).astype(BF16)
        key = recv[t, 512:640]
        ks[at] = key
        vs[at] = recv[t, 640:768]
        kt[:, at] = key.astype(F32).T.astype(BF16)
        low[:, at] = recv[t, 768:800]
        return 0

    for t in range(TILES):
        arrange(t, 0)
    q_up_here = q_up[:, pl.ds(pl.multiple_of(here * 256, 256), 256)]
    v_up_here = v_up[:, pl.ds(pl.multiple_of((here // 2) * 128, 128), 128)]
    base = SCALE * LOG2E

    def block_step(i, _):
        @pl.when(i * QB < length)
        def _():
            query = qs[i]
            grad = gs[i]

            def first(start, size, carry, diagonal=False):
                peak, total, weighted = carry
                at = pl.ds(start, size)
                s = nt(ks[at], query) * base
                dp = nt(vs[at], grad)
                if diagonal:
                    ki = lax.broadcasted_iota(jnp.int32, (size, 2 * QB), 0) + (start - i * QB)
                    qi = lax.broadcasted_iota(jnp.int32, (size, 2 * QB), 1) & (QB - 1)
                    s = jnp.where(ki <= qi, s, FAR_BELOW)
                s_all[at] = s
                dp_all[at] = dp
                new = jnp.maximum(peak, jnp.max(s, 0, keepdims=True))
                e = jnp.exp2(s - new)
                alpha = jnp.exp2(peak - new)
                total = total * alpha + jnp.sum(e, 0, keepdims=True)
                weighted = weighted * alpha + jnp.sum(e * dp, 0, keepdims=True)
                return new, total, weighted

            zero = jnp.zeros((1, 2 * QB), F32)
            carry = (jnp.full((1, 2 * QB), FAR_BELOW, F32), zero, zero)
            sizes = [(a, min(KB, i * QB - a)) for a in range(0, i * QB, KB)]
            last = [(a, min(KB, QB)) for a in range(i * QB, i * QB + QB, min(KB, QB))]
            for start, size in sizes:
                carry = first(start, size, carry)
            for start, size in last:
                carry = first(start, size, carry, True)
            peak, total, weighted = carry
            lse = peak + jnp.log2(total)
            delta = weighted / total

            def second(start, size, dq):
                at = pl.ds(start, size)
                prob = jnp.exp2(s_all[at] - lse)
                grad_logit = (prob * (dp_all[at] - delta)).astype(BF16)
                if start >= i * QB:
                    dv[at] = nn(prob.astype(BF16), grad)
                    dk[at] = nn(grad_logit, query)
                else:
                    dv[at] += nn(prob.astype(BF16), grad)
                    dk[at] += nn(grad_logit, query)
                return dq + nn(kt[:, at], grad_logit)

            dq = jnp.zeros((128, 2 * QB), F32)
            for start, size in sizes + last:
                dq = second(start, size, dq)
            dq = dq * SCALE
            span = pl.ds(pl.multiple_of(i * QB, QB), QB)
            cosine, sine = rotary(tables, 2 * i, 2)
            for h in range(2):
                a = dq[0:64, h * QB : h * QB + QB]
                b = dq[64:128, h * QB : h * QB + QB]
                pre[h * 128 : h * 128 + 64, span] = (a * cosine + b * sine).astype(BF16)
                pre[h * 128 + 64 : h * 128 + 128, span] = (b * cosine - a * sine).astype(BF16)
                for half in range(2):
                    at = h * QB + half * TILE
                    out[inv[2 * i + half], h * 128 : h * 128 + 128] = dq[
                        :, at : at + TILE
                    ].astype(BF16)

        @pl.when(i * QB >= length)
        def _():
            span = pl.ds(i * QB, QB)
            for half in range(2):
                out[inv[2 * i + half], 0:256] = jnp.zeros((256, 128), BF16)
            dk[span] = jnp.zeros((QB, 128), F32)
            dv[span] = jnp.zeros((QB, 128), F32)
            pre[:, span] = jnp.zeros((256, QB), BF16)

        return 0

    for i in range(BLOCKS):
        block_step(i, 0)

    grad_value = dv[...].astype(BF16)
    inner[0:R] = nn(q_up_here, pre[...]).astype(BF16)
    inner[R : 2 * R] = nt(v_up_here, grad_value).astype(BF16)
    up_q = nt(low[0:R], pre[...])
    upg[0:R] = up_q[:, 0:128]
    upg[R : 2 * R] = up_q[:, 128:256]
    upg[2 * R : 3 * R] = nn(low[R : 2 * R], grad_value)
    for p in range(TILES):
        at = slice(p * TILE, p * TILE + TILE)
        t = inv[p]
        out[t, 256:384] = (dk[at] * SCALE).astype(BF16)
        out[t, 384:512] = dv[at].astype(BF16)
        out[t, 512:544] = inner[:, at]
    up_out[...] = upg[...] * ADAPTER_SCALING


def rotary_tables():
    half = DH // 2
    freq = np.exp(-np.arange(half, dtype=np.float32) * np.float32(math.log(500000.0) / half))
    freq = freq.astype(np.float64)[:, None]
    row = freq * np.arange(TILE)[None, :]
    start = freq * (np.arange(TILE)[None, :] * TILE)
    return np.concatenate([np.cos(row), np.sin(row), np.cos(start), np.sin(start)], 0).astype(
        np.float32
    )


def attention(place, info, recv, q_up, v_up):
    tables = rotary_tables()
    return pl.pallas_call(
        attention_kernel,
        out_shape=(
            jax.ShapeDtypeStruct((TILES, OUT_ROWS, 128), BF16),
            jax.ShapeDtypeStruct((3 * R, 128), F32),
        ),
        in_specs=[SMEM, SMEM] + [VMEM] * 4,
        out_specs=(VMEM, VMEM),
        scratch_shapes=[
            pltpu.VMEM((BLOCKS, 2 * QB, 128), BF16),
            pltpu.VMEM((BLOCKS, 2 * QB, 128), BF16),
            pltpu.VMEM((WINDOW, 128), BF16),
            pltpu.VMEM((WINDOW, 128), BF16),
            pltpu.VMEM((128, WINDOW), BF16),
            pltpu.VMEM((2 * R, WINDOW), BF16),
            pltpu.VMEM((WINDOW, 2 * QB), F32),
            pltpu.VMEM((WINDOW, 2 * QB), F32),
            pltpu.VMEM((WINDOW, 128), F32),
            pltpu.VMEM((WINDOW, 128), F32),
            pltpu.VMEM((2 * R, WINDOW), BF16),
            pltpu.VMEM((2 * DH, WINDOW), BF16),
            pltpu.VMEM((3 * R, 128), F32),
            pltpu.SMEM((TILES,), jnp.int32),
        ],
        compiler_params=params(36),
        name="attention",
    )(place, info, recv, q_up, v_up, tables)


def down_kernel(back, features, out):
    inner = jnp.sum(back[:, 512:544].astype(F32), 0).astype(BF16)
    down = nn(inner, features[...]) * ADAPTER_SCALING
    for j in range(TILES):
        for half in range(2):
            at = j * 256 + half * 128
            out[j, half * 32 : half * 32 + 32] = down[:, at : at + 128].astype(BF16)


def down(back, features):
    return pl.pallas_call(
        down_kernel,
        out_shape=jax.ShapeDtypeStruct((TILES, 4 * R, 128), BF16),
        in_specs=[VMEM] * 2,
        out_specs=VMEM,
        compiler_params=params(24),
        name="down",
    )(back, features)


def chain_kernel(parts, ups, out):
    piece = jnp.sum(parts[...].astype(F32), 0).astype(BF16)
    up = ups[...].astype(BF16)
    for c in range(DP):
        out[c, 0 : 4 * R] = piece
        out[c, 4 * R : PIECE] = up


def chain_sum(parts, ups):
    return pl.pallas_call(
        chain_kernel,
        out_shape=jax.ShapeDtypeStruct((DP, PIECE, 128), BF16),
        in_specs=[VMEM] * 2,
        out_specs=VMEM,
        compiler_params=params(16),
        name="chain_sum",
    )(parts, ups)


def all_kernel(parts, out):
    piece = jnp.sum(parts[...].astype(F32), 0).astype(BF16)
    for j in range(TILES):
        out[j] = piece


def all_sum(parts):
    return pl.pallas_call(
        all_kernel,
        out_shape=jax.ShapeDtypeStruct((TILES, PIECE, 128), BF16),
        in_specs=[VMEM],
        out_specs=VMEM,
        compiler_params=params(16),
        name="all_sum",
    )(parts)


def unpack_kernel(back, grad_query, grad_key, grad_value):
    for j in range(TILES):
        grad_query[:, j * 256 : j * 256 + 128] = back[j, 0:128].astype(F32).T.astype(BF16)
        grad_query[:, j * 256 + 128 : j * 256 + 256] = back[j, 128:256].astype(F32).T.astype(BF16)
    for h in range(KVH):
        at = slice(h * 128, h * 128 + 128)
        grad_key[:, at] = (
            back[2 * h, 256:384].astype(F32) + back[2 * h + 1, 256:384].astype(F32)
        ).astype(BF16)
        grad_value[:, at] = (
            back[2 * h, 384:512].astype(F32) + back[2 * h + 1, 384:512].astype(F32)
        ).astype(BF16)


def unpack(back):
    return pl.pallas_call(
        unpack_kernel,
        out_shape=(
            jax.ShapeDtypeStruct((TILE, H * DH), BF16),
            jax.ShapeDtypeStruct((TILE, KVH * DH), BF16),
            jax.ShapeDtypeStruct((TILE, KVH * DH), BF16),
        ),
        in_specs=[VMEM],
        out_specs=(VMEM, VMEM, VMEM),
        compiler_params=params(24),
        name="unpack",
    )(back)


def final_kernel(pieces, q_down, q_up, v_down, v_up):
    for j in range(TILES):
        piece = pieces[j].astype(F32)
        for half in range(2):
            at = slice(j * 256 + half * 128, j * 256 + half * 128 + 128)
            q_down[:, at] = piece[half * 32 : half * 32 + R]
            v_down[:, at] = piece[half * 32 + R : half * 32 + 2 * R]
            q_up[:, at] = piece[4 * R + half * R : 5 * R + half * R]
    for h in range(KVH):
        v_up[:, h * 128 : h * 128 + 128] = pieces[2 * h, 6 * R : PIECE].astype(F32) + pieces[
            2 * h + 1, 6 * R : PIECE
        ].astype(F32)


def final(pieces):
    return pl.pallas_call(
        final_kernel,
        out_shape=(
            jax.ShapeDtypeStruct((R, D), F32),
            jax.ShapeDtypeStruct((R, H * DH), F32),
            jax.ShapeDtypeStruct((R, D), F32),
            jax.ShapeDtypeStruct((R, KVH * DH), F32),
        ),
        in_specs=[VMEM],
        out_specs=(VMEM,) * 4,
        compiler_params=params(24),
        name="final",
    )(pieces)


def exchange(array, axes):
    return lax.all_to_all(array, axes, 0, 0, tiled=True)


def body(
    features,
    queries,
    keys,
    values,
    grad_out,
    lengths,
    placement,
    query_down,
    query_up,
    value_down,
    value_up,
):
    here = lax.axis_index("ctx")
    info = jnp.stack([here.astype(jnp.int32), lengths[0]])
    packed = pack(
        info, features[0], queries[0], keys[0], values[0], grad_out[0], query_down.T, value_down.T
    )
    recv = exchange(packed, "ctx")
    out, ups = attention(placement[0], info, recv, query_up, value_up)
    back = exchange(out, "ctx")
    parts = exchange(down(back, features[0]), "ctx")
    parts = exchange(chain_sum(parts, ups), "dp")
    grad_query, grad_key, grad_value = unpack(back)
    pieces = exchange(all_sum(parts), "ctx")
    q_down, q_up, v_down, v_up = final(pieces)
    return (grad_query[None], grad_key[None], grad_value[None], q_down.T, q_up, v_down.T, v_up)


def solution(mesh):
    rows = P("dp", "ctx", None)
    return jax.shard_map(
        body,
        mesh=mesh,
        in_specs=(rows,) * 5 + (P("dp"), P("dp", None)) + (P(),) * 4,
        out_specs=(rows,) * 3 + (P(),) * 4,
        check_vma=False,
    )
```

profile of v0, /device:TPU:0, one launch (start us, length us, event | category | flops | bytes accessed | tf_op | source)
XLA Modules:
  0.0 140.0 jit_solution(14335575789192604286)
XLA Ops:
  1.3 0.6 pad_add_fusion.info
  1.9 4.2 %pack.1 = bf16[16,800,128]{2,1,0:T(8,128)(2,1)} custom-call(s32[2]{0:T(128)} %pad_add_fusion.info, bf16[128,4096]{1,0:T(8,128)(2,1)} %bitcast.14, bf16[128,4096]{1,0:T(8,128)(2,1)} %bitcast.17, bf16[128,1024]{1,0:T(8,128)(2,1)} %bitcast.19, bf16[128,1024]{1,0:T(8,128)(2,1)} %bitcast.20, bf16[128,4096]{1,0:T(8,128)(2,1)} %bitcast.18, ...), custom_call_target="tpu_custom_call" | custom-call | tf_op jit(solution)/shard_map/pack/pallas_call | solution.py:120
  6.1 0.0 copy-start.1
  6.1 0.0 copy-start.2
  6.1 0.0 copy-start.3
  6.1 0.0 copy-start.4
  6.1 0.0 copy-start.5
  6.2 49.4 %all_to_all.25.recv = bf16[16,800,128]{2,1,0:T(8,128)(2,1)S(1)} all-to-all(bf16[16,800,128]{2,1,0:T(8,128)(2,1)} %pack.1), channel_id=1, replica_groups=mesh['dp'=8,'ctx'=16] {'ctx'}, dimensions={0} | all-to-all | bytes 6553600 | tf_op jit(solution)/shard_map/all_to_all | solution.py:457
  55.5 0.0 copy-done.1
  55.5 0.0 copy-done.2
  55.5 0.0 copy-done.3
  55.5 0.0 copy-done.4
  55.6 0.0 copy-done.5
  55.6 0.0 copy-start
  55.6 18.4 %attention.1 = (bf16[16,544,128]{2,1,0:T(8,128)(2,1)S(1)}, f32[48,128]{1,0:T(8,128)S(1)}) custom-call(s32[16]{0:T(128)S(1)} %bitcast.16, s32[2]{0:T(128)S(1)} %copy-done.4, bf16[16,800,128]{2,1,0:T(8,128)(2,1)S(1)} %all_to_all.25.recv, bf16[16,4096]{1,0:T(8,128)(2,1)S(1)} %copy-done.1, bf16[16,1024]{1,0:T(8,128)(2,1)S(1)} %copy-done.3, f32[256,128]{1,0:T(8,128)S(1)} %copy-done.2), custom_call_target="tpu_custom_call" | custom-call | tf_op jit(solution)/shard_map/attention/pallas_call | solution.py:312
  74.0 24.6 %all_to_all.26.back = bf16[16,544,128]{2,1,0:T(8,128)(2,1)S(1)} all-to-all(bf16[16,544,128]{2,1,0:T(8,128)(2,1)S(1)} %get-tuple-element.16), channel_id=1, replica_groups=mesh['dp'=8,'ctx'=16] {'ctx'}, dimensions={0} | all-to-all | bytes 4456448 | tf_op jit(solution)/shard_map/all_to_all | solution.py:457
  98.6 0.3 down.1
  98.9 11.8 %all_to_all.27.parts = bf16[16,64,128]{2,1,0:T(8,128)(2,1)S(1)} all-to-all(bf16[16,64,128]{2,1,0:T(8,128)(2,1)S(1)} %down.1), channel_id=1, replica_groups=mesh['dp'=8,'ctx'=16] {'ctx'}, dimensions={0} | all-to-all | bytes 524288 | tf_op jit(solution)/shard_map/all_to_all | solution.py:457
  110.8 13.2 %all_to_all.28.parts = bf16[8,112,128]{2,1,0:T(8,128)(2,1)S(1)} all-to-all(bf16[8,112,128]{2,1,0:T(8,128)(2,1)S(1)} %chain_sum.1), channel_id=1, replica_groups=mesh['dp'=8,'ctx'=16] {'dp'}, dimensions={0} | all-to-all | bytes 458752 | tf_op jit(solution)/shard_map/all_to_all | solution.py:457
  124.0 0.8 all_sum.1
  124.8 3.6 %all-to-all-start.4 = ((bf16[16,112,128]{2,1,0:T(8,128)(2,1)}), bf16[16,112,128]{2,1,0:T(8,128)(2,1)S(1)}, u32[]{:S(2)}, u32[]{:S(2)}) async-start(bf16[16,112,128]{2,1,0:T(8,128)(2,1)} %all_sum.1), calls=%async_computation.4 | async-start | bytes 917504 | tf_op jit(solution)/shard_map/all_to_all | solution.py:457
  128.4 1.5 %unpack.1 = (bf16[128,4096]{1,0:T(8,128)(2,1)}, bf16[128,1024]{1,0:T(8,128)(2,1)}, bf16[128,1024]{1,0:T(8,128)(2,1)}) custom-call(bf16[16,544,128]{2,1,0:T(8,128)(2,1)S(1)} %all_to_all.26.back), custom_call_target="tpu_custom_call" | custom-call | tf_op jit(solution)/shard_map/unpack/pallas_call | solution.py:412
  129.9 9.2 %all-to-all-done.4.pieces = bf16[16,112,128]{2,1,0:T(8,128)(2,1)S(1)} async-done(((bf16[16,112,128]{2,1,0:T(8,128)(2,1)}), bf16[16,112,128]{2,1,0:T(8,128)(2,1)S(1)}, u32[]{:S(2)}, u32[]{:S(2)}) %all-to-all-start.4) | async-done | bytes 458784 | tf_op jit(solution)/shard_map/all_to_all | solution.py:457
  139.1 0.9 final.1
  (2 shorter events, 0.0 us)
Async XLA Ops:
  6.1 49.4 %copy-start.1 = (bf16[16,4096]{1,0:T(8,128)(2,1)S(1)}, bf16[16,4096]{1,0:T(8,128)(2,1)}, u32[]{:S(2)}) copy-start(bf16[16,4096]{1,0:T(8,128)(2,1)} %q_up.1) | copy-start | bytes 393220
  6.1 49.4 %copy-start.2 = (f32[256,128]{1,0:T(8,128)S(1)}, f32[256,128]{1,0:T(8,128)}, u32[]{:S(2)}) copy-start(f32[256,128]{1,0:T(8,128)} %constant.6.clone.tables) | copy-start | bytes 393220
  6.1 49.4 %copy-start.3 = (bf16[16,1024]{1,0:T(8,128)(2,1)S(1)}, bf16[16,1024]{1,0:T(8,128)(2,1)}, u32[]{:S(2)}) copy-start(bf16[16,1024]{1,0:T(8,128)(2,1)} %v_up.1) | copy-start | bytes 98308
  6.1 49.4 %copy-start.4 = (s32[2]{0:T(128)S(1)}, s32[2]{0:T(128)}, u32[]{:S(2)}) copy-start(s32[2]{0:T(128)} %pad_add_fusion.info) | copy-start | bytes 28
  6.1 49.4 %copy-start.5 = (s32[1,16]{1,0:T(1,128)S(1)}, s32[1,16]{1,0:T(1,128)}, u32[]{:S(2)}) copy-start(s32[1,16]{1,0:T(1,128)} %param.18) | copy-start | bytes 196
  55.6 43.0 %copy-start = (bf16[1,128,4096]{2,1,0:T(8,128)(2,1)S(1)}, bf16[1,128,4096]{2,1,0:T(8,128)(2,1)}, u32[]{:S(2)}) copy-start(bf16[1,128,4096]{2,1,0:T(8,128)(2,1)} %param.12) | copy-start | bytes 3145732
  124.8 14.3 %all-to-all-start.4 = ((bf16[16,112,128]{2,1,0:T(8,128)(2,1)}), bf16[16,112,128]{2,1,0:T(8,128)(2,1)S(1)}, u32[]{:S(2)}, u32[]{:S(2)}) async-start(bf16[16,112,128]{2,1,0:T(8,128)(2,1)} %all_sum.1), calls=%async_computation.4 | async-start | bytes 917504 | tf_op jit(solution)/shard_map/all_to_all | solution.py:457
where the time goes:
time: 140 us
  blocking collectives  99.1 us (71%)
  Pallas kernels  26.2 us (19%)
  waiting for transfers between devices  9.17 us (7%)
  starting transfers between devices  3.63 us (3%)
    all_to_all x4, blocking collectives, exchange(): return lax.all_to_all(array, axes, 0, 0, tiled=True)  99.1 us
    pallas_call x1, Pallas kernels, attention(): pl.pallas_call(attention_kernel, out_shape=(jax.ShapeDtypeStruct((TILES,...  18.4 us
    all_to_all x1, waiting for transfers between devices, exchange(): return lax.all_to_all(array, axes, 0, 0, tiled=True)  9.17 us
    pallas_call x1, Pallas kernels, pack(): pl.pallas_call(pack_kernel, out_shape=jax.ShapeDtypeStruct((TILES, IN_ROW...  4.22 us
    all_to_all x1, starting transfers between devices, exchange(): return lax.all_to_all(array, axes, 0, 0, tiled=True)  3.63 us
  transfers between devices with their start and end apart: 1, of which 1 were waited for; matrix products, arithmetic and copies ran while one was open for 0% of the time, Pallas kernels for 1%

commit v1 on v0

--- a/solution.py
+++ b/solution.py
@@ -51,7 +51,8 @@
 
 
 def pack_kernel(
-    info,
+    place,
+    lengths,
     features,
     queries,
     keys,
@@ -116,11 +117,11 @@
         made.wait()
 
 
-def pack(info, features, queries, keys, values, grad_out, q_down, v_down):
+def pack(place, lengths, features, queries, keys, values, grad_out, q_down, v_down):
     return pl.pallas_call(
         pack_kernel,
         out_shape=jax.ShapeDtypeStruct((TILES, IN_ROWS, 128), BF16),
-        in_specs=[SMEM] + [HBM] * 7,
+        in_specs=[SMEM] * 2 + [HBM] * 7,
         out_specs=HBM,
         scratch_shapes=[
             pltpu.VMEM((TILE, D), BF16),
@@ -135,7 +136,7 @@
         ],
         compiler_params=params(56),
         name="pack",
-    )(info, features, queries, keys, values, grad_out, q_down, v_down)
+    )(place, lengths, features, queries, keys, values, grad_out, q_down, v_down)
 
 
 def rotary(tables, tile, count):
@@ -150,7 +151,7 @@
 
 def attention_kernel(
     place,
-    info,
+    lengths,
     recv,
     q_up,
     v_up,
@@ -172,8 +173,8 @@
     upg,
     inv,
 ):
-    here = info[0]
-    length = info[1]
+    here = lax.axis_index("ctx")
+    length = lengths[0]
     rows = lax.broadcasted_iota(jnp.int32, (TILE, 128), 0)
 
     def arrange(t, _):
@@ -191,12 +192,15 @@
         key = recv[t, 512:640]
         ks[at] = key
         vs[at] = recv[t, 640:768]
-        kt[:, at] = key.astype(F32).T.astype(BF16)
         low[:, at] = recv[t, 768:800]
         return 0
 
     for t in range(TILES):
         arrange(t, 0)
+    one = lax.broadcasted_iota(jnp.int32, (128, 128), 0) == lax.broadcasted_iota(
+        jnp.int32, (128, 128), 1
+    )
+    kt[...] = nt(jnp.where(one, 1.0, 0.0).astype(BF16), ks[...]).astype(BF16)
     q_up_here = q_up[:, pl.ds(pl.multiple_of(here * 256, 256), 256)]
     v_up_here = v_up[:, pl.ds(pl.multiple_of((here // 2) * 128, 128), 128)]
     base = SCALE * LOG2E
@@ -307,7 +311,7 @@
     )
 
 
-def attention(place, info, recv, q_up, v_up):
+def attention(place, lengths, recv, q_up, v_up):
     tables = rotary_tables()
     return pl.pallas_call(
         attention_kernel,
@@ -335,7 +339,7 @@
         ],
         compiler_params=params(36),
         name="attention",
-    )(place, info, recv, q_up, v_up, tables)
+    )(place, lengths, recv, q_up, v_up, tables)
 
 
 def down_kernel(back, features, out):
@@ -470,13 +474,11 @@
     value_down,
     value_up,
 ):
-    here = lax.axis_index("ctx")
-    info = jnp.stack([here.astype(jnp.int32), lengths[0]])
     packed = pack(
-        info, features[0], queries[0], keys[0], values[0], grad_out[0], query_down.T, value_down.T
+        placement[0], lengths, features[0], queries[0], keys[0], values[0], grad_out[0], query_down.T, value_down.T
     )
     recv = exchange(packed, "ctx")
-    out, ups = attention(placement[0], info, recv, query_up, value_up)
+    out, ups = attention(placement[0], lengths, recv, query_up, value_up)
     back = exchange(out, "ctx")
     parts = exchange(down(back, features[0]), "ctx")
     parts = exchange(chain_sum(parts, ups), "dp")

time: 140 us -> 143 us (1.021)
  blocking collectives: 99.1 us -> 109 us
  Pallas kernels: 26.2 us -> 19.7 us
    all_to_all x4, blocking collectives: 99.1 us -> 109 us  [exchange(): return lax.all_to_all(array, axes, 0, 0, tiled=True)]
    pallas_call x1, Pallas kernels: 18.4 us -> 11.9 us  [attention(): pl.pallas_call(attention_kernel, out_shape=(jax.ShapeDtypeStruct((TILES,...]
where the time goes in v1:
time: 143 us
  blocking collectives  109 us (76%)
  Pallas kernels  19.7 us (14%)
  waiting for transfers between devices  9.12 us (6%)
  starting transfers between devices  3.67 us (3%)
    all_to_all x4, blocking collectives, exchange(): return lax.all_to_all(array, axes, 0, 0, tiled=True)  109 us
    pallas_call x1, Pallas kernels, attention(): pl.pallas_call(attention_kernel, out_shape=(jax.ShapeDtypeStruct((TILES,...  11.9 us
    all_to_all x1, waiting for transfers between devices, exchange(): return lax.all_to_all(array, axes, 0, 0, tiled=True)  9.12 us
    pallas_call x1, Pallas kernels, pack(): pl.pallas_call(pack_kernel, out_shape=jax.ShapeDtypeStruct((TILES, IN_ROW...  4.23 us
    all_to_all x1, starting transfers between devices, exchange(): return lax.all_to_all(array, axes, 0, 0, tiled=True)  3.67 us
  transfers between devices with their start and end apart: 1, of which 1 were waited for; matrix products, arithmetic and copies ran while one was open for 0% of the time, Pallas kernels for 1%

profile of v1, /device:TPU:0, one launch (start us, length us, event | category | flops | bytes accessed | tf_op | source)
XLA Modules:
  0.0 143.2 jit_solution(4998532596300076775)
XLA Ops:
  1.3 4.2 %pack.1 = bf16[16,800,128]{2,1,0:T(8,128)(2,1)} custom-call(s32[16]{0:T(128)} %bitcast.15, s32[1]{0:T(128)S(6)} %copy.19.lengths, bf16[128,4096]{1,0:T(8,128)(2,1)} %bitcast.13, bf16[128,4096]{1,0:T(8,128)(2,1)} %bitcast.17, bf16[128,1024]{1,0:T(8,128)(2,1)} %bitcast.19, bf16[128,1024]{1,0:T(8,128)(2,1)} %bitcast.20, bf16[128,4096]{1,0:T(8,128)(2,1)} %bitcast.18, ...), custom_call_target="tpu_custom_call" | custom-call | tf_op jit(solution)/shard_map/pack/pallas_call | solution.py:121
  5.5 0.0 copy-start.1
  5.5 0.0 copy-start.2
  5.5 0.0 copy-start.3
  5.6 0.0 copy-start.4
  5.6 49.4 %all_to_all.25.recv = bf16[16,800,128]{2,1,0:T(8,128)(2,1)S(1)} all-to-all(bf16[16,800,128]{2,1,0:T(8,128)(2,1)} %pack.1), channel_id=1, replica_groups=mesh['dp'=8,'ctx'=16] {'ctx'}, dimensions={0} | all-to-all | bytes 6553600 | tf_op jit(solution)/shard_map/all_to_all | solution.py:461
  54.9 0.0 copy-done.1
  54.9 0.0 copy-done.2
  55.0 0.0 copy-done.3
  55.0 0.0 copy-done.4
  55.0 0.0 copy-start
  55.0 11.9 %attention.1 = (bf16[16,544,128]{2,1,0:T(8,128)(2,1)S(1)}, f32[48,128]{1,0:T(8,128)S(1)}) custom-call(s32[16]{0:T(128)S(1)} %bitcast.16, s32[1]{0:T(128)S(6)} %copy.19.lengths, bf16[16,800,128]{2,1,0:T(8,128)(2,1)S(1)} %all_to_all.25.recv, bf16[16,4096]{1,0:T(8,128)(2,1)S(1)} %copy-done.1, bf16[16,1024]{1,0:T(8,128)(2,1)S(1)} %copy-done.3, ...), custom_call_target="tpu_custom_call" | custom-call | tf_op jit(solution)/shard_map/attention/pallas_call | solution.py:316
  66.9 34.0 %all_to_all.26.back = bf16[16,544,128]{2,1,0:T(8,128)(2,1)S(1)} all-to-all(bf16[16,544,128]{2,1,0:T(8,128)(2,1)S(1)} %get-tuple-element.16), channel_id=1, replica_groups=mesh['dp'=8,'ctx'=16] {'ctx'}, dimensions={0} | all-to-all | bytes 4456448 | tf_op jit(solution)/shard_map/all_to_all | solution.py:461
  100.9 0.0 copy-done
  100.9 0.3 down.1
  101.2 12.4 %all_to_all.27.parts = bf16[16,64,128]{2,1,0:T(8,128)(2,1)S(1)} all-to-all(bf16[16,64,128]{2,1,0:T(8,128)(2,1)S(1)} %down.1), channel_id=1, replica_groups=mesh['dp'=8,'ctx'=16] {'ctx'}, dimensions={0} | all-to-all | bytes 524288 | tf_op jit(solution)/shard_map/all_to_all | solution.py:461
  113.6 13.5 %all_to_all.28.parts = bf16[8,112,128]{2,1,0:T(8,128)(2,1)S(1)} all-to-all(bf16[8,112,128]{2,1,0:T(8,128)(2,1)S(1)} %chain_sum.1), channel_id=1, replica_groups=mesh['dp'=8,'ctx'=16] {'dp'}, dimensions={0} | all-to-all | bytes 458752 | tf_op jit(solution)/shard_map/all_to_all | solution.py:461
  127.2 0.8 all_sum.1
  128.0 3.7 %all-to-all-start.4 = ((bf16[16,112,128]{2,1,0:T(8,128)(2,1)}), bf16[16,112,128]{2,1,0:T(8,128)(2,1)S(1)}, u32[]{:S(2)}, u32[]{:S(2)}) async-start(bf16[16,112,128]{2,1,0:T(8,128)(2,1)} %all_sum.1), calls=%async_computation.4 | async-start | bytes 917504 | tf_op jit(solution)/shard_map/all_to_all | solution.py:461
  131.7 1.5 %unpack.1 = (bf16[128,4096]{1,0:T(8,128)(2,1)}, bf16[128,1024]{1,0:T(8,128)(2,1)}, bf16[128,1024]{1,0:T(8,128)(2,1)}) custom-call(bf16[16,544,128]{2,1,0:T(8,128)(2,1)S(1)} %all_to_all.26.back), custom_call_target="tpu_custom_call" | custom-call | tf_op jit(solution)/shard_map/unpack/pallas_call | solution.py:416
  133.2 9.1 %all-to-all-done.4.pieces = bf16[16,112,128]{2,1,0:T(8,128)(2,1)S(1)} async-done(((bf16[16,112,128]{2,1,0:T(8,128)(2,1)}), bf16[16,112,128]{2,1,0:T(8,128)(2,1)S(1)}, u32[]{:S(2)}, u32[]{:S(2)}) %all-to-all-start.4) | async-done | bytes 458784 | tf_op jit(solution)/shard_map/all_to_all | solution.py:461
  142.3 0.9 final.1
  (1 shorter events, 0.0 us)
Async XLA Ops:
  5.5 49.4 %copy-start.1 = (bf16[16,4096]{1,0:T(8,128)(2,1)S(1)}, bf16[16,4096]{1,0:T(8,128)(2,1)}, u32[]{:S(2)}) copy-start(bf16[16,4096]{1,0:T(8,128)(2,1)} %q_up.1) | copy-start | bytes 393220
  5.5 49.4 %copy-start.2 = (f32[256,128]{1,0:T(8,128)S(1)}, f32[256,128]{1,0:T(8,128)}, u32[]{:S(2)}) copy-start(f32[256,128]{1,0:T(8,128)} %constant.2.clone.tables) | copy-start | bytes 393220
  5.5 49.4 %copy-start.3 = (bf16[16,1024]{1,0:T(8,128)(2,1)S(1)}, bf16[16,1024]{1,0:T(8,128)(2,1)}, u32[]{:S(2)}) copy-start(bf16[16,1024]{1,0:T(8,128)(2,1)} %v_up.1) | copy-start | bytes 98308
  5.6 49.4 %copy-start.4 = (s32[1,16]{1,0:T(1,128)S(1)}, s32[1,16]{1,0:T(1,128)}, u32[]{:S(2)}) copy-start(s32[1,16]{1,0:T(1,128)} %param.18) | copy-start | bytes 196
  55.0 45.9 %copy-start = (bf16[1,128,4096]{2,1,0:T(8,128)(2,1)S(1)}, bf16[1,128,4096]{2,1,0:T(8,128)(2,1)}, u32[]{:S(2)}) copy-start(bf16[1,128,4096]{2,1,0:T(8,128)(2,1)} %param.12) | copy-start | bytes 3145732
  128.0 14.3 %all-to-all-start.4 = ((bf16[16,112,128]{2,1,0:T(8,128)(2,1)}), bf16[16,112,128]{2,1,0:T(8,128)(2,1)S(1)}, u32[]{:S(2)}, u32[]{:S(2)}) async-start(bf16[16,112,128]{2,1,0:T(8,128)(2,1)} %all_sum.1), calls=%async_computation.4 | async-start | bytes 917504 | tf_op jit(solution)/shard_map/all_to_all | solution.py:461

commit v2 on v1

--- a/solution.py
+++ b/solution.py
@@ -26,7 +26,7 @@
 OUT_ROWS = 4 * TILE + 2 * R
 PIECE = 7 * R
 PARTS = 4
-PACK_COPIES = 3 * PARTS + 6
+PACK_COPIES = 3 * PARTS + 5
 QB = 256
 KB = 256
 BLOCKS = WINDOW // QB
@@ -80,6 +80,7 @@
 
     width = D // PARTS
     some = TILES // PARTS
+    low = [copy(features, f_in), copy(q_down, qd_in), copy(v_down, vd_in)]
     waits = [copy(keys, k_in), copy(values, v_in)]
     parts = []
     for p in range(PARTS):
@@ -87,7 +88,13 @@
         parts.append(
             (copy(queries.at[:, at], q_in.at[:, at]), copy(grad_out.at[:, at], g_in.at[:, at]))
         )
-    low = [copy(features, f_in), copy(q_down, qd_in), copy(v_down, vd_in)]
+    for made in low:
+        made.wait()
+    low_q = nt(qd_in[...], f_in[...]).astype(BF16)
+    low_v = nt(vd_in[...], f_in[...]).astype(BF16)
+    for j in range(TILES):
+        held[j, 768:784] = low_q
+        held[j, 784:800] = low_v
     for made in waits:
         made.wait()
     sent = []
@@ -102,17 +109,8 @@
             held[j, 384:512] = g_in[:, j * 256 + 128 : j * 256 + 256]
             held[j, 512:640] = k_in[:, h * 128 : h * 128 + 128]
             held[j, 640:768] = v_in[:, h * 128 : h * 128 + 128]
-        at = pl.ds(p * some, some), pl.ds(0, 6 * TILE)
+        at = pl.ds(p * some, some)
         sent.append(copy(held.at[at], out.at[at]))
-    for made in low:
-        made.wait()
-    low_q = nt(qd_in[...], f_in[...]).astype(BF16)
-    low_v = nt(vd_in[...], f_in[...]).astype(BF16)
-    for j in range(TILES):
-        held[j, 768:784] = low_q
-        held[j, 784:800] = low_v
-    at = pl.ds(0, TILES), pl.ds(6 * TILE, 2 * R)
-    sent.append(copy(held.at[at], out.at[at]))
     for made in sent:
         made.wait()
 

time: 143 us -> 139 us (0.972)
  Pallas kernels: 19.7 us -> 17.5 us
  blocking collectives: 109 us -> 107 us
    pallas_call x1, Pallas kernels: 11.9 us -> 9.41 us  [attention(): pl.pallas_call(attention_kernel, out_shape=(jax.ShapeDtypeStruct((TILES,...]
    all_to_all x4, blocking collectives: 109 us -> 107 us  [exchange(): return lax.all_to_all(array, axes, 0, 0, tiled=True)]
where the time goes in v2:
time: 139 us
  blocking collectives  107 us (77%)
  Pallas kernels  17.5 us (13%)
  waiting for transfers between devices  9.12 us (7%)
  starting transfers between devices  3.67 us (3%)
    all_to_all x4, blocking collectives, exchange(): return lax.all_to_all(array, axes, 0, 0, tiled=True)  107 us
    pallas_call x1, Pallas kernels, attention(): pl.pallas_call(attention_kernel, out_shape=(jax.ShapeDtypeStruct((TILES,...  9.41 us
    all_to_all x1, waiting for transfers between devices, exchange(): return lax.all_to_all(array, axes, 0, 0, tiled=True)  9.12 us
    pallas_call x1, Pallas kernels, pack(): pl.pallas_call(pack_kernel, out_shape=jax.ShapeDtypeStruct((TILES, IN_ROW...  4.56 us
    all_to_all x1, starting transfers between devices, exchange(): return lax.all_to_all(array, axes, 0, 0, tiled=True)  3.67 us
  transfers between devices with their start and end apart: 1, of which 1 were waited for; matrix products, arithmetic and copies ran while one was open for 0% of the time, Pallas kernels for 1%

profile of v2, /device:TPU:0, one launch (start us, length us, event | category | flops | bytes accessed | tf_op | source)
XLA Modules:
  0.0 138.8 jit_solution(16606711235774932150)
XLA Ops:
  1.3 4.6 %pack.1 = bf16[16,800,128]{2,1,0:T(8,128)(2,1)} custom-call(s32[16]{0:T(128)} %bitcast.15, s32[1]{0:T(128)S(6)} %copy.19.lengths, bf16[128,4096]{1,0:T(8,128)(2,1)} %bitcast.13, bf16[128,4096]{1,0:T(8,128)(2,1)} %bitcast.17, bf16[128,1024]{1,0:T(8,128)(2,1)} %bitcast.19, bf16[128,1024]{1,0:T(8,128)(2,1)} %bitcast.20, bf16[128,4096]{1,0:T(8,128)(2,1)} %bitcast.18, ...), custom_call_target="tpu_custom_call" | custom-call | tf_op jit(solution)/shard_map/pack/pallas_call | solution.py:119
  5.8 0.0 copy-start.1
  5.9 0.0 copy-start.2
  5.9 0.0 copy-start.3
  5.9 0.0 copy-start.4
  5.9 49.4 %all_to_all.25.recv = bf16[16,800,128]{2,1,0:T(8,128)(2,1)S(1)} all-to-all(bf16[16,800,128]{2,1,0:T(8,128)(2,1)} %pack.1), channel_id=1, replica_groups=mesh['dp'=8,'ctx'=16] {'ctx'}, dimensions={0} | all-to-all | bytes 6553600 | tf_op jit(solution)/shard_map/all_to_all | solution.py:459
  55.3 0.0 copy-done.1
  55.3 0.0 copy-done.2
  55.3 0.0 copy-done.3
  55.3 0.0 copy-done.4
  55.3 0.0 copy-start
  55.3 9.4 %attention.1 = (bf16[16,544,128]{2,1,0:T(8,128)(2,1)S(1)}, f32[48,128]{1,0:T(8,128)S(1)}) custom-call(s32[16]{0:T(128)S(1)} %bitcast.16, s32[1]{0:T(128)S(6)} %copy.19.lengths, bf16[16,800,128]{2,1,0:T(8,128)(2,1)S(1)} %all_to_all.25.recv, bf16[16,4096]{1,0:T(8,128)(2,1)S(1)} %copy-done.1, bf16[16,1024]{1,0:T(8,128)(2,1)S(1)} %copy-done.3, ...), custom_call_target="tpu_custom_call" | custom-call | tf_op jit(solution)/shard_map/attention/pallas_call | solution.py:314
  64.7 28.3 %all_to_all.26.back = bf16[16,544,128]{2,1,0:T(8,128)(2,1)S(1)} all-to-all(bf16[16,544,128]{2,1,0:T(8,128)(2,1)S(1)} %get-tuple-element.16), channel_id=1, replica_groups=mesh['dp'=8,'ctx'=16] {'ctx'}, dimensions={0} | all-to-all | bytes 4456448 | tf_op jit(solution)/shard_map/all_to_all | solution.py:459
  93.0 0.0 copy-done
  93.0 0.3 down.1
  93.3 12.1 %all_to_all.27.parts = bf16[16,64,128]{2,1,0:T(8,128)(2,1)S(1)} all-to-all(bf16[16,64,128]{2,1,0:T(8,128)(2,1)S(1)} %down.1), channel_id=1, replica_groups=mesh['dp'=8,'ctx'=16] {'ctx'}, dimensions={0} | all-to-all | bytes 524288 | tf_op jit(solution)/shard_map/all_to_all | solution.py:459
  105.4 17.4 %all_to_all.28.parts = bf16[8,112,128]{2,1,0:T(8,128)(2,1)S(1)} all-to-all(bf16[8,112,128]{2,1,0:T(8,128)(2,1)S(1)} %chain_sum.1), channel_id=1, replica_groups=mesh['dp'=8,'ctx'=16] {'dp'}, dimensions={0} | all-to-all | bytes 458752 | tf_op jit(solution)/shard_map/all_to_all | solution.py:459
  122.8 0.8 all_sum.1
  123.6 3.7 %all-to-all-start.4 = ((bf16[16,112,128]{2,1,0:T(8,128)(2,1)}), bf16[16,112,128]{2,1,0:T(8,128)(2,1)S(1)}, u32[]{:S(2)}, u32[]{:S(2)}) async-start(bf16[16,112,128]{2,1,0:T(8,128)(2,1)} %all_sum.1), calls=%async_computation.4 | async-start | bytes 917504 | tf_op jit(solution)/shard_map/all_to_all | solution.py:459
  127.3 1.5 %unpack.1 = (bf16[128,4096]{1,0:T(8,128)(2,1)}, bf16[128,1024]{1,0:T(8,128)(2,1)}, bf16[128,1024]{1,0:T(8,128)(2,1)}) custom-call(bf16[16,544,128]{2,1,0:T(8,128)(2,1)S(1)} %all_to_all.26.back), custom_call_target="tpu_custom_call" | custom-call | tf_op jit(solution)/shard_map/unpack/pallas_call | solution.py:414
  128.7 9.1 %all-to-all-done.4.pieces = bf16[16,112,128]{2,1,0:T(8,128)(2,1)S(1)} async-done(((bf16[16,112,128]{2,1,0:T(8,128)(2,1)}), bf16[16,112,128]{2,1,0:T(8,128)(2,1)S(1)}, u32[]{:S(2)}, u32[]{:S(2)}) %all-to-all-start.4) | async-done | bytes 458784 | tf_op jit(solution)/shard_map/all_to_all | solution.py:459
  137.9 0.9 final.1
  (1 shorter events, 0.0 us)
Async XLA Ops:
  5.8 49.4 %copy-start.1 = (bf16[16,4096]{1,0:T(8,128)(2,1)S(1)}, bf16[16,4096]{1,0:T(8,128)(2,1)}, u32[]{:S(2)}) copy-start(bf16[16,4096]{1,0:T(8,128)(2,1)} %q_up.1) | copy-start | bytes 393220
  5.9 49.4 %copy-start.2 = (f32[256,128]{1,0:T(8,128)S(1)}, f32[256,128]{1,0:T(8,128)}, u32[]{:S(2)}) copy-start(f32[256,128]{1,0:T(8,128)} %constant.2.clone.tables) | copy-start | bytes 393220
  5.9 49.4 %copy-start.3 = (bf16[16,1024]{1,0:T(8,128)(2,1)S(1)}, bf16[16,1024]{1,0:T(8,128)(2,1)}, u32[]{:S(2)}) copy-start(bf16[16,1024]{1,0:T(8,128)(2,1)} %v_up.1) | copy-start | bytes 98308
  5.9 49.4 %copy-start.4 = (s32[1,16]{1,0:T(1,128)S(1)}, s32[1,16]{1,0:T(1,128)}, u32[]{:S(2)}) copy-start(s32[1,16]{1,0:T(1,128)} %param.18) | copy-start | bytes 196
  55.3 37.7 %copy-start = (bf16[1,128,4096]{2,1,0:T(8,128)(2,1)S(1)}, bf16[1,128,4096]{2,1,0:T(8,128)(2,1)}, u32[]{:S(2)}) copy-start(bf16[1,128,4096]{2,1,0:T(8,128)(2,1)} %param.12) | copy-start | bytes 3145732
  123.6 14.3 %all-to-all-start.4 = ((bf16[16,112,128]{2,1,0:T(8,128)(2,1)}), bf16[16,112,128]{2,1,0:T(8,128)(2,1)S(1)}, u32[]{:S(2)}, u32[]{:S(2)}) async-start(bf16[16,112,128]{2,1,0:T(8,128)(2,1)} %all_sum.1), calls=%async_computation.4 | async-start | bytes 917504 | tf_op jit(solution)/shard_map/all_to_all | solution.py:459
